TPU v7x, 512 devices: a whole 4x4x16 slice. The times are simulated.
512 devices in a mesh: sub: 8 (over y, z_hi), row: 8 (over z_lo), col: 8 (over x, core).
Axes of the slice: x: 4, y: 4, z: 16 (z_hi: 2, z_lo: 8; z = z_hi * 8 + z_lo), core: 2. Of those that a mesh axis runs over, the one named last changes fastest.
Arguments:
- root_inverse: float32 [8192, 8192], P(('sub', 'row'), 'col')
- panel: float32 [8192, 2048], P(('sub', 'row'), 'col'), may hold values from -0.125 to 0.125
- pattern: int32 [64, 16], P(('sub', 'row'), 'col'), may hold values from 0 to 1, as said below
- diag_inverse: float32 [2048, 2048], P(('sub', 'row'), 'col')
Outputs:
- off_block: float32 [8192, 2048], P(('sub', 'row'), 'col')
- diag_block: float32 [2048, 2048], P(('sub', 'row'), 'col')
Inputs may be any that keep to these rules, and one draw needn't show every extreme that they name: `pattern`: in every tile row, each aligned group of 2 tile columns (those of one index of col) has exactly one tile marked 1.
All inputs are finite; a program needn't handle non-finite values.
Results may differ from a plain program's by a relative error of at most 0.000078.
Values sent between devices are 32-bit elements; how exact they have to be, the bound alone decides.
A program may use at most 64 MiB of HBM per device.

v0:
```python
import jax
import jax.numpy as jnp
from jax import lax
from jax.sharding import PartitionSpec as P

highest = lax.Precision.HIGHEST


def rows_of_inverse(root_inverse):
    return lax.all_gather(root_inverse, "col", axis=1, tiled=True)


def local(root_inverse, panel, pattern, diag_inverse):
    tile_rows = panel.shape[0]
    marked = pattern[0].astype(jnp.float32)
    column_mask = jnp.repeat(marked, tile_rows)
    masked_panel = panel * column_mask[None, :]
    inverse_full = rows_of_inverse(root_inverse)
    accumulated = jnp.dot(
        inverse_full,
        lax.all_gather(masked_panel, ("sub", "row"), axis=0, tiled=True),
        precision=highest,
        preferred_element_type=jnp.float32,
    )
    off_block = -(accumulated * column_mask[None, :])
    panel_full_row = lax.all_gather(masked_panel, "col", axis=1, tiled=True)
    contribution = lax.dot_general(
        panel_full_row,
        off_block,
        (((0,), (0,)), ((), ())),
        precision=highest,
        preferred_element_type=jnp.float32,
    )
    update = lax.psum_scatter(contribution, ("sub", "row"), scatter_dimension=0, tiled=True)
    diag_block = diag_inverse - update
    return (off_block, diag_block)


def solution(mesh):
    in_specs = (
        P(("sub", "row"), "col"),
        P(("sub", "row"), "col"),
        P(("sub", "row"), "col"),
        P(("sub", "row"), "col"),
    )
    out_specs = (P(("sub", "row"), "col"), P(("sub", "row"), "col"))
    return jax.shard_map(local, mesh=mesh, in_specs=in_specs, out_specs=out_specs, check_vma=False)
```

profile of v0, /device:TPU:2, one launch (start us, length us, event | category | flops | bytes accessed | tf_op | source)
XLA Modules:
  0.0 950.3 jit_solution(14879854118065150119)
XLA Ops:
  7.2 0.0 all-gather.6.cloned.1.call-start
  7.2 0.7 all-gather.6.cloned.1.call-update
  7.9 0.0 all-gather.4.cloned.1.call-start
  7.9 0.7 convert_bitcast_fusion
  8.6 0.1 broadcast_bitcast_fusion
  8.7 1.6 broadcast_multiply_fusion
  10.2 0.0 all-gather.4.cloned.1.call-update
  10.3 0.0 all-gather.8.cloned.1.call-start
  10.3 0.7 all-gather.8.cloned.1.call-update
  11.0 0.0 reduce-scatter.2.cloned.1.call-start
  11.1 42.3 %all-gather.6.cloned.1.call-done = f32[128,8192]{1,0:T(8,128)} async-done(((f32[128,1024]{1,0:T(8,128)}), f32[128,8192]{1,0:T(8,128)}) %all-gather.6.cloned.1.call-update) | async-done | bytes 4194320 | tf_op jit(solution)/shard_map/all_gather | solution.py:10
  53.4 161.6 %all-gather.4.cloned.1.call-done = f32[8192,256]{1,0:T(8,128)} async-done(((f32[128,256]{1,0:T(8,128)}), f32[8192,256]{1,0:T(8,128)}) %all-gather.4.cloned.1.call-update) | async-done | bytes 8388624 | tf_op jit(solution)/shard_map/all_gather | solution.py:21
  215.0 16.3 %fusion = f32[256,128]{1,0:T(8,128)S(1)} fusion(f32[8192,256]{1,0:T(8,128)} %all-gather.4.cloned.1.call-done, f32[128,8192]{1,0:T(8,128)} %all-gather.6.cloned.1.call-done, f32[256]{0:T(256)S(1)} %broadcast_bitcast_fusion), kind=kOutput, calls=%fused_computation.1 | convolution fusion | flops 3221291008 | bytes 12715008 | tf_op jit(solution)/shard_map/dot_general | solution.py:19
  231.3 0.0 copy-start
  231.3 11.0 %all-gather.8.cloned.1.call-done = f32[128,2048]{1,0:T(8,128)} async-done(((f32[128,256]{1,0:T(8,128)}), f32[128,2048]{1,0:T(8,128)}) %all-gather.8.cloned.1.call-update) | async-done | bytes 1048592 | tf_op jit(solution)/shard_map/all_gather | solution.py:26
  242.3 4.4 fusion.1
  246.7 0.0 reduce-scatter.2.cloned.1.call-update
  246.7 0.8 copy.6
  247.5 694.9 %reduce-scatter.2.cloned.1.call-done = f32[32,256]{1,0:T(8,128)} async-done(((f32[2048,256]{1,0:T(8,128)}), f32[32,256]{1,0:T(8,128)}) %reduce-scatter.2.cloned.1.call-update) | async-done | bytes 32784 | tf_op jit(solution)/shard_map/reduce_scatter | solution.py:34
  942.4 0.0 copy-done
  942.4 1.4 sub.3
Async XLA Ops:
  7.2 46.2 %all-gather.6.cloned.1.call-start = ((), (), s32[]{:S(2)}) async-start(), calls=%async_computation.2 | async-start | bytes 4718592 | tf_op jit(solution)/shard_map/all_gather | solution.py:10
  7.9 207.1 %all-gather.4.cloned.1.call-start = ((), (), s32[]{:S(2)}) async-start(), calls=%async_computation.1 | async-start | bytes 8519680 | tf_op jit(solution)/shard_map/all_gather | solution.py:21
  10.3 232.0 %all-gather.8.cloned.1.call-start = ((), (), s32[]{:S(2)}) async-start(), calls=%async_computation.3 | async-start | bytes 1179648 | tf_op jit(solution)/shard_map/all_gather | solution.py:26
  11.0 931.4 %reduce-scatter.2.cloned.1.call-start = ((), (), s32[]{:S(2)}) async-start(), calls=%async_computation.4 | async-start | bytes 2129920 | tf_op jit(solution)/shard_map/reduce_scatter | solution.py:34
  231.3 711.1 %copy-start = (f32[32,256]{1,0:T(8,128)S(1)}, f32[32,256]{1,0:T(8,128)}, u32[]{:S(2)}) copy-start(f32[32,256]{1,0:T(8,128)} %param.7) | copy-start | bytes 98308
Sparse Core Ops, SparseCore 0:
  10.1 43.1 all-gather.5
  56.9 158.0 all-gather.3
  217.7 24.5 all-gather.7
  246.8 695.4 reduce-scatter.1
where the time goes:
time: 951 us; the launch traced here: 950 us
  waiting for transfers between devices  911 us (96%)
  matrix products  20.7 us (2%)
  between operations  13.8 us (1%)
    reduce_scatter x1, waiting for transfers between devices, local(): lax.psum_scatter(contribution, ('sub', 'row'), scatter_dimension=0, tiled...  695 us
    all_gather x1, waiting for transfers between devices, local(): lax.all_gather(masked_panel, ('sub', 'row'), axis=0, tiled=True)  162 us
    all_gather x1, waiting for transfers between devices, rows_of_inverse(): return lax.all_gather(root_inverse, 'col', axis=1, tiled=True)  42.3 us
  transfers between devices with their start and end apart: 4, of which 4 were waited for; matrix products, arithmetic and copies ran while one was open for 2% of the time, Pallas kernels for 0%

commit v1 on v0

--- a/solution.py
+++ b/solution.py
@@ -6,8 +6,30 @@
 highest = lax.Precision.HIGHEST
 
 
+def in_order(blocks, dim):
+    blocks = jnp.moveaxis(blocks, 0, dim)
+    shape = blocks.shape
+    return blocks.reshape(*shape[:dim], shape[dim] * shape[dim + 1], *shape[dim + 2 :])
+
+
+def ring_gather(array, axis, dim):
+    size = lax.axis_size(axis)
+    pairs = [(i, (i + 1) % size) for i in range(size)]
+    back = [(b, a) for a, b in pairs]
+    lower, upper = ([], [])
+    for step in range(size - 1):
+        if step % 2 == 0:
+            lower.append(lax.ppermute(lower[-1] if lower else array, axis, pairs))
+        else:
+            upper.append(lax.ppermute(upper[-1] if upper else array, axis, back))
+    parts = jnp.stack([*lower[::-1], array, *upper])
+    shift = lax.axis_index(axis) - len(lower)
+    parts = parts[(jnp.arange(size) - shift) % size]
+    return in_order(parts, dim)
+
+
 def rows_of_inverse(root_inverse):
-    return lax.all_gather(root_inverse, "col", axis=1, tiled=True)
+    return ring_gather(root_inverse, "col", 1)
 
 
 def local(root_inverse, panel, pattern, diag_inverse):

time: 951 us -> 908 us (0.955)
  the two profiles are of different devices: /device:TPU:2 before, /device:TPU:4 now
where the time goes in v1:
time: 908 us; the launch traced here: 907 us
  waiting for transfers between devices  850 us (94%)
  local copies, waits for them, and re-layouts  18.3 us (2%)
  matrix products  15.9 us (2%)
  between operations  13.8 us (2%)
    reduce_scatter x1, waiting for transfers between devices, local(): lax.psum_scatter(contribution, ('sub', 'row'), scatter_dimension=0, tiled...  695 us
    all_gather x1, waiting for transfers between devices, local(): lax.all_gather(masked_panel, ('sub', 'row'), axis=0, tiled=True)  110 us
    ppermute x4, waiting for transfers between devices, ring_gather(): lower.append(lax.ppermute(lower[-1] if lower else array, axis, pairs))  28.7 us
  transfers between devices with their start and end apart: 10, of which 8 were waited for; matrix products, arithmetic and copies ran while one was open for 3% of the time, Pallas kernels for 0%

profile of v1, /device:TPU:4, one launch (start us, length us, event | category | flops | bytes accessed | tf_op | source)
XLA Modules:
  0.0 907.2 jit_solution(11375981855370127096)
XLA Ops:
  7.2 0.0 copy-start.1
  7.2 0.0 all-gather.3.cloned.1.call-start
  7.2 0.7 convert_bitcast_fusion
  7.9 0.1 broadcast_bitcast_fusion
  8.0 1.6 broadcast_multiply_fusion
  9.6 0.0 all-gather.3.cloned.1.call-update
  9.6 0.0 all-gather.5.cloned.1.call-start
  9.7 0.0 collective-permute-start
  9.7 8.8 collective-permute-done
  18.5 0.0 collective-permute-start.1
  18.5 1.7 collective-permute-start.4
  20.2 6.9 collective-permute-done.1
  27.1 0.0 collective-permute-start.2
  27.1 0.2 collective-permute-done.4
  27.2 1.8 collective-permute-start.5
  29.0 6.6 collective-permute-done.2
  35.7 0.0 collective-permute-start.3
  35.7 0.0 all-gather.5.cloned.1.call-update
  35.7 0.0 reduce-scatter.2.cloned.1.call-start
  35.8 0.0 collective-permute-done.5
  35.8 2.2 collective-permute-start.6
  38.0 6.4 collective-permute-done.3
  44.4 1.9 bitcast_dynamic-update-slice_fusion.7
  46.3 0.9 bitcast_dynamic-update-slice_fusion.6
  47.2 0.8 bitcast_dynamic-update-slice_fusion.5
  48.0 0.9 bitcast_dynamic-update-slice_fusion.4
  48.9 0.0 copy-done.1
  48.9 0.8 bitcast_dynamic-update-slice_fusion.3
  49.7 0.8 bitcast_dynamic-update-slice_fusion.2
  50.6 0.8 bitcast_dynamic-update-slice_fusion.1
  51.4 0.0 collective-permute-done.6
  51.4 0.8 bitcast_dynamic-update-slice_fusion
  52.2 5.0 gather_fusion
  57.2 5.4 copy.6
  62.6 109.8 %all-gather.3.cloned.1.call-done = f32[8192,256]{1,0:T(8,128)} async-done(((f32[128,256]{1,0:T(8,128)}), f32[8192,256]{1,0:T(8,128)}) %all-gather.3.cloned.1.call-update) | async-done | bytes 8388624 | tf_op jit(solution)/shard_map/all_gather | solution.py:43
  172.4 11.5 %fusion = f32[128,256]{1,0:T(8,128)S(1)} fusion(f32[128,8192]{0,1:T(8,128)} %bitcast.28, f32[8192,256]{1,0:T(8,128)} %all-gather.3.cloned.1.call-done, f32[256]{0:T(256)S(1)} %broadcast_bitcast_fusion), kind=kOutput, calls=%fused_computation.2 | convolution fusion | flops 3221291008 | bytes 12715008 | tf_op jit(solution)/shard_map/dot_general | solution.py:41
  183.9 0.0 copy-start
  183.9 0.0 copy-start.2
  183.9 15.5 %all-gather.5.cloned.1.call-done = f32[128,2048]{1,0:T(8,128)} async-done(((f32[128,256]{1,0:T(8,128)}), f32[128,2048]{1,0:T(8,128)}) %all-gather.5.cloned.1.call-update) | async-done | bytes 1048592 | tf_op jit(solution)/shard_map/all_gather | solution.py:48
  199.4 4.4 fusion.3
  203.8 0.0 reduce-scatter.2.cloned.1.call-update
  203.8 695.5 %reduce-scatter.2.cloned.1.call-done = f32[32,256]{1,0:T(8,128)} async-done(((f32[2048,256]{1,0:T(8,128)}), f32[32,256]{1,0:T(8,128)}) %reduce-scatter.2.cloned.1.call-update) | async-done | bytes 32784 | tf_op jit(solution)/shard_map/reduce_scatter | solution.py:56
  899.3 0.0 copy-done.2
  899.3 1.4 sub.22
  900.7 0.0 copy-done
  (2 shorter events, 0.0 us)
Async XLA Ops:
  7.2 41.7 %copy-start.1 = (f32[128,1024]{1,0:T(8,128)S(1)}, f32[128,1024]{1,0:T(8,128)}, u32[]{:S(2)}) copy-start(f32[128,1024]{1,0:T(8,128)} %param.4) | copy-start | bytes 1572868
  7.2 165.2 %all-gather.3.cloned.1.call-start = ((), (), s32[]{:S(2)}) async-start(), calls=%async_computation.1 | async-start | bytes 8519680 | tf_op jit(solution)/shard_map/all_gather | solution.py:43
  9.6 189.8 %all-gather.5.cloned.1.call-start = ((), (), s32[]{:S(2)}) async-start(), calls=%async_computation.2 | async-start | bytes 1179648 | tf_op jit(solution)/shard_map/all_gather | solution.py:48
  9.7 8.8 collective-permute-start
  18.5 8.6 collective-permute-start.1
  18.5 8.8 collective-permute-start.4
  27.1 8.6 collective-permute-start.2
  27.2 8.6 collective-permute-start.5
  35.7 8.7 collective-permute-start.3
  35.7 863.6 %reduce-scatter.2.cloned.1.call-start = ((), (), s32[]{:S(2)}) async-start(), calls=%async_computation.3 | async-start | bytes 2129920 | tf_op jit(solution)/shard_map/reduce_scatter | solution.py:56
  35.8 15.6 %collective-permute-start.6 = (f32[128,1024]{1,0:T(8,128)S(1)}, f32[128,1024]{1,0:T(8,128)S(1)}, u32[]{:S(2)}, u32[]{:S(2)}) collective-permute-start(f32[128,1024]{1,0:T(8,128)S(1)} %collective-permute-done.5), channel_id=1, source_target_pairs={{1,0},{2,1},{3,2},{4,3},{5,4},{6,5},{7,6},{0,7},{9,8},{10,9},{11,1... | collective-permute-start | bytes 1572872 | tf_op jit(solution)/shard_map/ppermute | solution.py:24
  183.9 716.7 %copy-start = (f32[128,256]{1,0:T(8,128)}, f32[128,256]{1,0:T(8,128)S(1)}, u32[]{:S(2)}) copy-start(f32[128,256]{1,0:T(8,128)S(1)} %fusion) | copy-start | bytes 393220
  183.9 715.3 %copy-start.2 = (f32[32,256]{1,0:T(8,128)S(1)}, f32[32,256]{1,0:T(8,128)}, u32[]{:S(2)}) copy-start(f32[32,256]{1,0:T(8,128)} %param.7) | copy-start | bytes 98308
Sparse Core Ops, SparseCore 0:
  11.0 161.3 all-gather.2
  174.5 24.8 all-gather.4
  203.9 695.2 reduce-scatter.1
